TPU v7x, 32 devices: a whole 2x2x4 slice. The times are simulated.
32 devices in a mesh: img: 8 (over z, core), seq: 4 (over y, x).
Axes of the slice: x: 2, y: 2, z: 4, core: 2. Of those that a mesh axis runs over, the one named last changes fastest.
Arguments:
- patches: bfloat16 [8, 4096, 512], P('img', 'seq'), may hold values from -40 to 40
- router: bfloat16 [512, 64], replicated, may hold values from -3 to 3
- w_in: bfloat16 [8, 4096, 512], P('seq', 'img'), may hold values from -0.25 to 0.25
- w_out: bfloat16 [8, 4096, 512], P('seq', 'img'), may hold values from -0.09375 to 0.09375
- cotangent: bfloat16 [8, 4096, 512], P('img', 'seq'), may hold values from -6 to 6
Outputs:
- patch_grad: bfloat16 [8, 4096, 512], P('img', 'seq')
- router_grad: bfloat16 [512, 64], replicated
- w_in_grad: bfloat16 [8, 4096, 512], P('seq', 'img')
- w_out_grad: bfloat16 [8, 4096, 512], P('seq', 'img')
All inputs are finite; a program needn't handle non-finite values.
Results may differ from a plain program's by a relative error of at most 0.03.
Values may be sent and summed in bfloat16 or wider, within the bound.
A program may use at most 64 MiB of HBM per device.

v0:
```python
import math

import jax
import jax.numpy as jnp
from jax import lax
from jax.sharding import PartitionSpec as P

D = 512
SLOTS = 8


def gelu_slope(values):
    coeff = math.sqrt(2.0 / math.pi)
    inside = coeff * (values + 0.044715 * values * values * values)
    tangent = jnp.tanh(inside)
    return 0.5 * (1.0 + tangent) + 0.5 * values * (1.0 - tangent * tangent) * coeff * (
        1.0 + 3.0 * 0.044715 * values * values
    )


def local(patches, router, w_in, w_out, cotangent):
    expert_count = w_in.shape[0]
    owned_rows = expert_count * SLOTS
    logits = jnp.einsum("bpd,dn->bpn", patches, router, preferred_element_type=jnp.float32)
    highest = lax.pmax(jnp.max(logits, axis=1), "seq")
    raised = jnp.exp(logits - highest[:, None, :])
    totals = lax.psum(jnp.sum(raised, axis=1), "seq")
    dispatch = (raised / totals[:, None, :]).astype(jnp.bfloat16)
    combine = jax.nn.softmax(logits, axis=-1).astype(jnp.bfloat16)
    partial_in = jnp.einsum("bpn,bpd->bnd", dispatch, patches, preferred_element_type=jnp.float32)
    summed_in = lax.psum(partial_in.astype(jnp.bfloat16), "seq").astype(jnp.float32)
    slot_in = lax.dynamic_slice_in_dim(summed_in, lax.axis_index("seq") * owned_rows, owned_rows, 1)
    slot_in = slot_in.astype(jnp.bfloat16)
    every_in = lax.all_gather(slot_in, "img", axis=0, tiled=True)
    image_count = every_in.shape[0]
    grouped = every_in.reshape(image_count, expert_count, SLOTS, D)
    hidden = jnp.einsum("besd,efd->besf", grouped, w_in, preferred_element_type=jnp.float32)
    active = jax.nn.gelu(hidden, approximate=True).astype(jnp.bfloat16)
    block_rows = active
    result = jnp.einsum("besf,efd->besd", block_rows, w_out, preferred_element_type=jnp.float32)
    slot_out = lax.psum_scatter(
        result.reshape(patches.shape[0] * lax.axis_size("img"), owned_rows, D).astype(jnp.bfloat16),
        "img",
        scatter_dimension=0,
        tiled=True,
    )
    every_out = lax.all_gather(slot_out, "seq", axis=1, tiled=True)
    comb_grad = jnp.einsum("bpd,bnd->bpn", cotangent, every_out, preferred_element_type=jnp.float32)
    partial_grad = jnp.einsum(
        "bpn,bpd->bnd", combine, cotangent, preferred_element_type=jnp.float32
    )
    summed_grad = lax.psum(partial_grad.astype(jnp.bfloat16), "seq").astype(jnp.float32)
    slot_grad = lax.dynamic_slice_in_dim(
        summed_grad, lax.axis_index("seq") * owned_rows, owned_rows, 1
    )
    slot_grad = slot_grad.astype(jnp.bfloat16)
    every_grad = lax.all_gather(slot_grad, "img", axis=0, tiled=True)
    grad_four = every_grad.reshape(image_count, expert_count, SLOTS, D)
    act_grad = jnp.einsum("besd,efd->besf", grad_four, w_out, preferred_element_type=jnp.float32)
    hidden_grad = (act_grad * gelu_slope(hidden)).astype(jnp.bfloat16)
    w_out_grad = jnp.einsum(
        "besf,besd->efd", active, grad_four, preferred_element_type=jnp.float32
    ).astype(jnp.bfloat16)
    w_in_grad = jnp.einsum(
        "besf,besd->efd", hidden_grad, grouped, preferred_element_type=jnp.float32
    ).astype(jnp.bfloat16)
    block_rows = hidden_grad
    result = jnp.einsum("besf,efd->besd", block_rows, w_in, preferred_element_type=jnp.float32)
    input_grad = lax.psum_scatter(
        result.reshape(patches.shape[0] * lax.axis_size("img"), owned_rows, D).astype(jnp.bfloat16),
        "img",
        scatter_dimension=0,
        tiled=True,
    )
    every_input = lax.all_gather(input_grad, "seq", axis=1, tiled=True)
    disp_grad = jnp.einsum("bpd,bnd->bpn", patches, every_input, preferred_element_type=jnp.float32)
    disp_wide = dispatch.astype(jnp.float32)
    comb_wide = combine.astype(jnp.float32)
    inner_sum = lax.psum(jnp.sum(disp_wide * disp_grad, axis=1), "seq")
    across = jnp.sum(comb_wide * comb_grad, axis=-1, keepdims=True)
    logit_grad = (
        disp_wide * (disp_grad - inner_sum[:, None, :]) + comb_wide * (comb_grad - across)
    ).astype(jnp.bfloat16)
    first_term = jnp.einsum("bpn,dn->bpd", logit_grad, router, preferred_element_type=jnp.float32)
    second_term = jnp.einsum(
        "bpn,bnd->bpd", dispatch, every_input, preferred_element_type=jnp.float32
    )
    patch_grad = (first_term + second_term).astype(jnp.bfloat16)
    router_part = jnp.einsum("bpd,bpn->dn", patches, logit_grad, preferred_element_type=jnp.float32)
    router_grad = lax.psum(router_part, ("img", "seq")).astype(jnp.bfloat16)
    return (patch_grad, router_grad, w_in_grad, w_out_grad)


def solution(mesh):
    placed = (
        P("img", "seq", None),
        P(),
        P("seq", "img", None),
        P("seq", "img", None),
        P("img", "seq", None),
    )
    return jax.shard_map(
        local,
        mesh=mesh,
        in_specs=placed,
        out_specs=(P("img", "seq", None), P(), P("seq", "img", None), P("seq", "img", None)),
        check_vma=False,
    )
```

profile of v0, /device:TPU:0, one launch (start us, length us, event | category | flops | bytes accessed | tf_op | source)
XLA Modules:
  0.0 225.2 jit_solution(9154067009326829449)
XLA Ops:
  7.2 1.2 copy-done
  8.4 1.4 fusion.46
  9.8 11.5 %pmax.7 = f32[64]{0:T(128)S(1)} all-reduce(f32[64]{0:T(128)S(1)} %get-tuple-element.7), channel_id=1, replica_groups=mesh['img'=8,'seq'=4] {'seq'}, use_global_device_ids=true, to_apply=%region_1.0 | all-reduce | flops 64 | bytes 512 | tf_op jit(solution)/shard_map/pmax | solution.py:25
  21.5 8.0 %psum.35 = f32[64]{0:T(128)S(1)} all-reduce(f32[64]{0:T(128)S(1)} %get-tuple-element.5), channel_id=1, replica_groups=mesh['img'=8,'seq'=4] {'seq'}, use_global_device_ids=true, to_apply=%region_3.0 | all-reduce | flops 64 | bytes 512 | tf_op jit(solution)/shard_map/psum | solution.py:27
  29.6 0.9 fusion.6
  30.6 0.9 fusion.5
  31.6 42.5 %all-reduce.4.cloned.1.call-done = (bf16[1,64,512]{2,1,0:T(8,128)(2,1)}, bf16[1,64,512]{2,1,0:T(8,128)(2,1)}) async-done(((bf16[1,64,512]{2,1,0:T(8,128)(2,1)}, bf16[1,64,512]{2,1,0:T(8,128)(2,1)}), (bf16[1,64,512]{2,1,0:T(8,128)(2,1)}, bf16[1,64,512]{2,1,0:T(8,128)(2,1)})) %all-reduce.4.cloned.1.call-update) | async-done | bytes 131088 | tf_op jit(solution)/shard_map/psum | solution.py:31
  74.0 0.8 convert_convert_fusion
  74.9 14.1 %all_gather.13 = bf16[8,16,512]{2,1,0:T(8,128)(2,1)S(1)} all-gather(bf16[1,16,512]{2,1,0:T(8,128)(2,1)S(1)} %convert_convert_fusion), channel_id=1, replica_groups=mesh['img'=8,'seq'=4] {'img'}, dimensions={0}, use_global_device_ids=true | all-gather | bytes 147456 | tf_op jit(solution)/shard_map/all_gather | solution.py:34
  88.9 0.7 convert_convert_fusion.1
  89.6 14.0 %all_gather.12 = bf16[8,16,512]{2,1,0:T(8,128)(2,1)S(1)} all-gather(bf16[1,16,512]{2,1,0:T(8,128)(2,1)S(1)} %convert_convert_fusion.1), channel_id=1, replica_groups=mesh['img'=8,'seq'=4] {'img'}, dimensions={0}, use_global_device_ids=true | all-gather | bytes 147456 | tf_op jit(solution)/shard_map/all_gather | solution.py:57
  104.1 1.5 fusion.4
  106.0 1.5 bitcast_convert_fusion
  107.8 0.7 copy.42
  108.6 0.6 copy.41
  109.2 2.4 %bitcast_convert_fusion.1 = bf16[2,512,512]{2,1,0:T(8,128)(2,1)} fusion(bf16[8,2,8,512]{3,2,0,1:T(8,128)(2,1)} %copy-done.7, bf16[8,16,512]{2,1,0:T(8,128)(2,1)S(1)} %all_gather.13), kind=kOutput, calls=%fused_computation.1 | convolution fusion | flops 67633152 | bytes 1310720 | tf_op jit(solution)/shard_map/besf,besd->efd/dot_general | solution.py:64
  111.6 27.0 %reduce-scatter.3.cloned.1.call-done = bf16[1,16,512]{2,1,0:T(8,128)(2,1)} async-done(((bf16[8,16,512]{2,1,0:T(8,128)(2,1)}), bf16[1,16,512]{2,1,0:T(8,128)(2,1)}) %reduce-scatter.3.cloned.1.call-update) | async-done | bytes 16400 | tf_op jit(solution)/shard_map/reduce_scatter | solution.py:69
  138.6 8.4 %all_gather.14 = bf16[1,64,512]{2,1,0:T(8,128)(2,1)S(1)} all-gather(bf16[1,16,512]{2,1,0:T(8,128)(2,1)} %reduce-scatter.3.cloned.1.call-done), channel_id=1, replica_groups=mesh['img'=8,'seq'=4] {'seq'}, dimensions={1}, use_global_device_ids=true | all-gather | bytes 81920 | tf_op jit(solution)/shard_map/all_gather | solution.py:75
  147.1 0.5 fusion.18
  147.6 8.9 %psum.38 = f32[64]{0:T(128)S(1)} all-reduce(f32[64]{0:T(128)S(1)} %get-tuple-element.15), channel_id=1, replica_groups=mesh['img'=8,'seq'=4] {'seq'}, use_global_device_ids=true, to_apply=%region_10.0 | all-reduce | flops 64 | bytes 512 | tf_op jit(solution)/shard_map/psum | solution.py:79
  156.5 12.7 %reduce-scatter.5.cloned.1.call-done = bf16[1,16,512]{2,1,0:T(8,128)(2,1)} async-done(((bf16[8,16,512]{2,1,0:T(8,128)(2,1)}), bf16[1,16,512]{2,1,0:T(8,128)(2,1)}) %reduce-scatter.5.cloned.1.call-update) | async-done | bytes 16400 | tf_op jit(solution)/shard_map/reduce_scatter | solution.py:41
  169.2 8.3 %all_gather.15 = bf16[1,64,512]{2,1,0:T(8,128)(2,1)S(1)} all-gather(bf16[1,16,512]{2,1,0:T(8,128)(2,1)} %reduce-scatter.5.cloned.1.call-done), channel_id=1, replica_groups=mesh['img'=8,'seq'=4] {'seq'}, dimensions={1}, use_global_device_ids=true | all-gather | bytes 81920 | tf_op jit(solution)/shard_map/all_gather | solution.py:47
  178.9 1.4 fusion
  180.3 38.3 %all-reduce.5 = bf16[512,64]{0,1:T(8,128)(2,1)} all-reduce(f32[512,64]{0,1:T(8,128)S(1)} %convolution_bitcast_fusion.4), channel_id=1, replica_groups=mesh['img'=8,'seq'=4] {'img','seq'}, use_global_device_ids=true, to_apply=%region_13.0 | all-reduce | flops 32768 | bytes 196608 | tf_op jit(solution)/shard_map/psum | solution.py:90
  (30 shorter events, 3.0 us)
Async XLA Ops:
  7.2 1.2 copy-start
  7.2 23.4 %copy-start.2 = (bf16[1,1024,512]{2,1,0:T(8,128)(2,1)S(1)}, bf16[1,1024,512]{2,1,0:T(8,128)(2,1)}, u32[]{:S(2)}) copy-start(bf16[1,1024,512]{2,1,0:T(8,128)(2,1)} %param.9) | copy-start | bytes 3145732
  7.2 66.9 %all-reduce.4.cloned.1.call-start = ((), (), s32[]{:S(2)}) async-start(), calls=%async_computation.4 | async-start | bytes 262144 | tf_op jit(solution)/shard_map/psum | solution.py:31
  9.8 93.9 %copy-start.1 = (bf16[2,512,512]{2,1,0:T(8,128)(2,1)S(1)}, bf16[2,512,512]{2,1,0:T(8,128)(2,1)}, u32[]{:S(2)}) copy-start(bf16[2,512,512]{2,1,0:T(8,128)(2,1)} %param.7) | copy-start | bytes 3145732
  29.6 0.9 copy-start.3
  31.5 107.1 %reduce-scatter.3.cloned.1.call-start = ((), (), s32[]{:S(2)}) async-start(), calls=%async_computation.2 | async-start | bytes 147456 | tf_op jit(solution)/shard_map/reduce_scatter | solution.py:69
  74.0 31.6 %copy-start.5 = (bf16[2,512,512]{2,1,0:T(8,128)(2,1)S(1)}, bf16[2,512,512]{2,1,0:T(8,128)(2,1)}, u32[]{:S(2)}) copy-start(bf16[2,512,512]{2,1,0:T(8,128)(2,1)} %param.8) | copy-start | bytes 3145732
  106.0 1.5 copy-start.7
  108.5 60.7 %reduce-scatter.5.cloned.1.call-start = ((), (), s32[]{:S(2)}) async-start(), calls=%async_computation.3 | async-start | bytes 147456 | tf_op jit(solution)/shard_map/reduce_scatter | solution.py:41
  109.2 68.3 %copy-start.4 = (bf16[1024,64]{0,1:T(8,128)(2,1)S(1)}, bf16[1024,64]{0,1:T(8,128)(2,1)}, u32[]{:S(2)}) copy-start(bf16[1024,64]{0,1:T(8,128)(2,1)} %copy-done.3) | copy-start | bytes 393220
  111.6 66.5 %copy-start.6 = (bf16[512,64]{0,1:T(8,128)(2,1)S(1)}, bf16[512,64]{0,1:T(8,128)(2,1)}, u32[]{:S(2)}) copy-start(bf16[512,64]{0,1:T(8,128)(2,1)} %param.6) | copy-start | bytes 196612
Sparse Core Ops, SparseCore 0:
  31.6 42.3 all-reduce.3
  108.6 29.9 reduce-scatter.2
  140.9 28.2 reduce-scatter.4
where the time goes:
time: 226 us; the launch traced here: 225 us
  blocking collectives  112 us (50%)
  waiting for transfers between devices  82.2 us (36%)
  between operations  13.9 us (6%)
  matrix products  12.9 us (6%)
  local copies, waits for them, and re-layouts  2.51 us (1%)
    psum x1, waiting for transfers between devices, local(): lax.psum(partial_in.astype(jnp.bfloat16), 'seq').astype(jnp.float32)  42.5 us
    reduce_scatter x2, waiting for transfers between devices, local(): lax.psum_scatter(result.reshape(patches.shape[0] * lax.axis_size('img'),...  39.7 us
    psum x1, blocking collectives, local(): router_grad = lax.psum(router_part, ('img', 'seq')).astype(jnp.bfloat16)  38.3 us
    all_gather x1, blocking collectives, local(): every_in = lax.all_gather(slot_in, 'img', axis=0, tiled=True)  14.1 us
    all_gather x1, blocking collectives, local(): every_grad = lax.all_gather(slot_grad, 'img', axis=0, tiled=True)  14 us
    pmax x1, blocking collectives, local(): highest = lax.pmax(jnp.max(logits, axis=1), 'seq')  11.5 us
    psum x1, blocking collectives, local(): inner_sum = lax.psum(jnp.sum(disp_wide * disp_grad, axis=1), 'seq')  8.93 us
    all_gather x1, blocking collectives, local(): every_input = lax.all_gather(input_grad, 'seq', axis=1, tiled=True)  8.42 us
  transfers between devices with their start and end apart: 3, of which 3 were waited for; matrix products, arithmetic and copies ran while one was open for 2% of the time, Pallas kernels for 0%

commit v1 on v0

v1 whole, which is shorter than its diff:
```python
import functools
import math

import jax
import jax.numpy as jnp
from jax import lax
from jax.experimental import pallas as pl
from jax.experimental.pallas import tpu as pltpu
from jax.sharding import PartitionSpec as P

SLOTS = 8
MESH = pl.DeviceIdType.MESH
BF = jnp.bfloat16
F32 = jnp.float32
MAX_LANE, TOTAL_LANE, INNER_LANE = 0, 1, 2


def dot(a, b, contract):
    return lax.dot_general(a, b, (contract, ((), ())), preferred_element_type=F32)


def gelu_and_slope(values):
    coeff = math.sqrt(2.0 / math.pi)
    square = values * values
    tangent = jnp.tanh(coeff * values * (1.0 + 0.044715 * square))
    half = 0.5 * (1.0 + tangent)
    slope = half + 0.5 * values * (1.0 - tangent * tangent) * coeff * (1.0 + 3.0 * 0.044715 * square)
    return values * half, slope


class Exchange:
    def __init__(self, axis, count, send_sem, recv_sem):
        self.axis, self.count = axis, count
        self.send_sem, self.recv_sem = send_sem, recv_sem
        self.me = lax.axis_index(axis)
        self.copies = []

    def start(self, source, landing, source_is_own):
        for step in range(1, self.count):
            peer = lax.rem(self.me + step, self.count)
            copy = pltpu.make_async_remote_copy(
                src_ref=source.at[self.me if source_is_own else peer],
                dst_ref=landing.at[self.me],
                send_sem=self.send_sem.at[step],
                recv_sem=self.recv_sem.at[step],
                device_id={self.axis: peer},
                device_id_type=MESH,
            )
            copy.start()
            self.copies.append(copy)

    def wait_recv(self):
        for copy in self.copies:
            copy.wait_recv()

    def wait_send(self):
        for copy in self.copies:
            copy.wait_send()


def kernel(
    n_img, n_seq,
    pat_hbm, rou_hbm, win_hbm, wout_hbm, cot_hbm,
    pg_hbm, rg_hbm, wig_hbm, wog_hbm,
    pat, rou, win, wout, cot,
    pg, rg, wig, wog,
    a_in_s, a_in_r, a_gr_s, a_gr_r, a_st_s, a_st_r,
    b_in, b_gr, c_out_s, c_out_r, c_ig_s, c_ig_r,
    d_out, d_ig, d_st, e_s, e_r, f_buf, g_buf,
    act_s, hg_s,
    load_sem, store_sem, seq_send, seq_recv, img_send, img_recv,
):
    img, seq = lax.axis_index("img"), lax.axis_index("seq")
    experts = win.shape[0]
    rows, depth = b_in.shape[1], b_in.shape[2]
    slots = n_seq * rows

    loads = []
    for at, (src, dst) in enumerate(
        ((pat_hbm.at[0], pat), (rou_hbm, rou), (cot_hbm.at[0], cot), (win_hbm, win), (wout_hbm, wout))
    ):
        copy = pltpu.make_async_copy(src, dst, load_sem.at[at])
        copy.start()
        loads.append(copy)

    barrier = pltpu.get_barrier_semaphore()
    for step in range(1, n_seq):
        pl.semaphore_signal(
            barrier, inc=1, device_id={"seq": lax.rem(seq + step, n_seq)}, device_id_type=MESH
        )
    for step in range(1, n_img):
        pl.semaphore_signal(
            barrier, inc=1, device_id={"img": lax.rem(img + step, n_img)}, device_id_type=MESH
        )

    def over_seq(at):
        return Exchange("seq", n_seq, seq_send.at[at], seq_recv.at[at])

    def over_img(at):
        return Exchange("img", n_img, img_send.at[at], img_recv.at[at])

    started = []

    def go(exchange, source, landing, own):
        exchange.start(source, landing, own)
        started.append(exchange)
        return exchange

    loads[1].wait()
    router_t = rou[...].astype(F32).T.astype(BF)
    loads[0].wait()
    logits = dot(router_t, pat[...], ((1,), (1,)))
    own_max = jnp.max(logits, axis=1, keepdims=True)
    raised = jnp.exp(logits - own_max)
    own_total = jnp.sum(raised, axis=1, keepdims=True)
    part_in = dot((raised * (1.0 / own_total)).astype(BF), pat[...], ((1,), (0,)))
    lane = lax.broadcasted_iota(jnp.int32, (slots, 128), 1)
    a_st_s[...] = jnp.where(lane == MAX_LANE, own_max, own_total).reshape(n_seq, rows, 128)
    a_in_s[...] = part_in.astype(BF).reshape(n_seq, rows, depth)
    a_st_r[seq] = a_st_s[seq]
    a_in_r[seq] = a_in_s[seq]
    pl.semaphore_wait(barrier, n_seq - 1 + n_img - 1)
    a_st = go(over_seq(0), a_st_s, a_st_r, False)
    a_in = go(over_seq(1), a_in_s, a_in_r, False)

    comb = jnp.exp(logits - jnp.max(logits, axis=0, keepdims=True))
    comb = comb * (1.0 / jnp.sum(comb, axis=0, keepdims=True))
    loads[2].wait()
    part_gr = dot(comb.astype(BF), cot[...], ((1,), (0,)))
    a_gr_s[...] = part_gr.astype(BF).reshape(n_seq, rows, depth)
    a_gr_r[seq] = a_gr_s[seq]
    a_gr = go(over_seq(2), a_gr_s, a_gr_r, False)

    a_st.wait_recv()
    a_in.wait_recv()
    stats = a_st_r[...]
    maxes, totals = stats[:, :, MAX_LANE:MAX_LANE + 1], stats[:, :, TOTAL_LANE:TOTAL_LANE + 1]
    top = jnp.max(maxes, axis=0, keepdims=True)
    shares = totals * jnp.exp(maxes - top)
    total = jnp.sum(shares, axis=0, keepdims=True)
    slot_in = jnp.sum(a_in_r[...].astype(F32) * (shares / total), axis=0)
    b_in[img] = slot_in.astype(BF)
    g_in = go(over_img(0), b_in, b_in, True)
    a_gr.wait_recv()
    b_gr[img] = jnp.sum(a_gr_r[...].astype(F32), axis=0).astype(BF)
    g_gr = go(over_img(1), b_gr, b_gr, True)

    def of_expert(buffer, e):
        wide = buffer[...].astype(F32).reshape(n_img, experts, SLOTS, depth)
        return wide[:, e].reshape(n_img * SLOTS, depth).astype(BF)

    def all_rows(parts):
        wide = [part.reshape(n_img, 1, SLOTS, depth) for part in parts]
        return jnp.concatenate(wide, axis=1).reshape(n_img, rows, depth).astype(BF)

    loads[3].wait()
    g_in.wait_recv()
    slopes, parts = [], []
    loads[4].wait()
    for e in range(experts):
        hidden = dot(of_expert(b_in, e), win[e], ((1,), (1,)))
        active, slope = gelu_and_slope(hidden)
        slopes.append(slope)
        act_s[e] = active.astype(BF)
        parts.append(dot(act_s[e], wout[e], ((1,), (0,))))
    c_out_s[...] = all_rows(parts)
    c_out_r[img] = c_out_s[img]
    c_out = go(over_img(2), c_out_s, c_out_r, False)
    g_gr.wait_recv()
    parts = []
    for e in range(experts):
        act_grad = dot(of_expert(b_gr, e), wout[e], ((1,), (1,)))
        hg_s[e] = (act_grad * slopes[e]).astype(BF)
        parts.append(dot(hg_s[e], win[e], ((1,), (0,))))
    c_ig_s[...] = all_rows(parts)
    c_ig_r[img] = c_ig_s[img]
    c_ig = go(over_img(3), c_ig_s, c_ig_r, False)

    stores = []

    def store(src, dst):
        copy = pltpu.make_async_copy(src, dst, store_sem.at[len(stores)])
        copy.start()
        stores.append(copy)

    for e in range(experts):
        wog[e] = dot(act_s[e], of_expert(b_gr, e), ((0,), (0,))).astype(BF)
    store(wog, wog_hbm)

    c_out.wait_recv()
    d_out[seq] = jnp.sum(c_out_r[...].astype(F32), axis=0).astype(BF)
    e_out = go(over_seq(3), d_out, d_out, True)
    for e in range(experts):
        wig[e] = dot(hg_s[e], of_expert(b_in, e), ((0,), (0,))).astype(BF)
    store(wig, wig_hbm)
    c_ig.wait_recv()
    input_grad = jnp.sum(c_ig_r[...].astype(F32), axis=0).astype(BF)
    d_ig[seq] = input_grad
    e_ig = go(over_seq(4), d_ig, d_ig, True)
    inner = jnp.sum(slot_in * input_grad.astype(F32), axis=1, keepdims=True)
    lane = lax.broadcasted_iota(jnp.int32, (rows, 128), 1)
    d_st[seq] = jnp.where(lane == MAX_LANE, top[0], jnp.where(lane == TOTAL_LANE, total[0], inner))
    e_st = go(over_seq(5), d_st, d_st, True)

    e_out.wait_recv()
    comb_grad = dot(d_out[...].reshape(slots, depth), cot[...], ((1,), (1,)))
    across = jnp.sum(comb * comb_grad, axis=0, keepdims=True)
    comb_part = comb * (comb_grad - across)
    e_ig.wait_recv()
    every_ig = d_ig[...].reshape(slots, depth)
    disp_grad = dot(every_ig, pat[...], ((1,), (1,)))
    e_st.wait_recv()
    stats = d_st[...].reshape(slots, 128)
    scale = jnp.exp(own_max - stats[:, MAX_LANE:MAX_LANE + 1]) / stats[:, TOTAL_LANE:TOTAL_LANE + 1]
    disp = raised * scale
    logit_grad = (disp * (disp_grad - stats[:, INNER_LANE:INNER_LANE + 1]) + comb_part).astype(BF)

    e_s[...] = dot(logit_grad, pat[...], ((1,), (0,))).reshape(n_seq, rows, depth)
    e_r[seq] = e_s[seq]
    r_sum = go(over_seq(6), e_s, e_r, False)
    left = jnp.concatenate([logit_grad, disp.astype(BF)], axis=0)
    right = jnp.concatenate([router_t, every_ig], axis=0)
    pg[...] = dot(left, right, ((0,), (0,))).astype(BF)
    store(pg, pg_hbm.at[0])
    r_sum.wait_recv()
    f_buf[img] = jnp.sum(e_r[...], axis=0).astype(BF)
    r_all = go(over_img(4), f_buf, f_buf, True)
    r_all.wait_recv()
    g_buf[seq] = jnp.sum(f_buf[...].astype(F32), axis=0).astype(BF)
    r_back = go(over_seq(7), g_buf, g_buf, True)
    r_back.wait_recv()
    rg[...] = g_buf[...].astype(F32).reshape(slots, depth).T.astype(BF)
    store(rg, rg_hbm)
    for exchange in started:
        exchange.wait_send()
    for copy in stores:
        copy.wait()


def local(n_img, n_seq, patches, router, w_in, w_out, cotangent):
    _, count, depth = patches.shape
    experts, units, _ = w_in.shape
    rows = experts * SLOTS
    slots = n_seq * rows
    any_space = pl.BlockSpec(memory_space=pl.ANY)
    vmem = pltpu.VMEM
    by_seq, by_img = (n_seq, rows, depth), (n_img, rows, depth)
    return pl.pallas_call(
        functools.partial(kernel, n_img, n_seq),
        out_shape=(
            jax.ShapeDtypeStruct(patches.shape, BF),
            jax.ShapeDtypeStruct(router.shape, BF),
            jax.ShapeDtypeStruct(w_in.shape, BF),
            jax.ShapeDtypeStruct(w_out.shape, BF),
        ),
        in_specs=[any_space] * 5,
        out_specs=(any_space,) * 4,
        scratch_shapes=[
            vmem((count, depth), BF), vmem(router.shape, BF), vmem(w_in.shape, BF),
            vmem(w_out.shape, BF), vmem((count, depth), BF),
            vmem((count, depth), BF), vmem(router.shape, BF), vmem(w_in.shape, BF),
            vmem(w_out.shape, BF),
            vmem(by_seq, BF), vmem(by_seq, BF), vmem(by_seq, BF), vmem(by_seq, BF),
            vmem((n_seq, rows, 128), F32), vmem((n_seq, rows, 128), F32),
            vmem(by_img, BF), vmem(by_img, BF), vmem(by_img, BF), vmem(by_img, BF),
            vmem(by_img, BF), vmem(by_img, BF),
            vmem(by_seq, BF), vmem(by_seq, BF), vmem((n_seq, rows, 128), F32),
            vmem(by_seq, F32), vmem(by_seq, F32), vmem(by_img, BF), vmem(by_seq, BF),
            vmem((experts, n_img * SLOTS, units), BF), vmem((experts, n_img * SLOTS, units), BF),
            pltpu.SemaphoreType.DMA((5,)), pltpu.SemaphoreType.DMA((4,)),
            pltpu.SemaphoreType.DMA((8, n_seq)), pltpu.SemaphoreType.DMA((8, n_seq)),
            pltpu.SemaphoreType.DMA((5, n_img)), pltpu.SemaphoreType.DMA((5, n_img)),
        ],
        compiler_params=pltpu.CompilerParams(
            collective_id=0, has_side_effects=True, vmem_limit_bytes=48 * 1024 * 1024
        ),
    )(patches, router, w_in, w_out, cotangent)


def solution(mesh):
    placed = (
        P("img", "seq", None),
        P(),
        P("seq", "img", None),
        P("seq", "img", None),
        P("img", "seq", None),
    )
    return jax.shard_map(
        functools.partial(local, mesh.shape["img"], mesh.shape["seq"]),
        mesh=mesh,
        in_specs=placed,
        out_specs=(P("img", "seq", None), P(), P("seq", "img", None), P("seq", "img", None)),
        check_vma=False,
    )
```

time: 226 us -> 47.7 us (0.21)
  blocking collectives: 112 us -> 0 us
  waiting for transfers between devices: 82.2 us -> 0 us
  Pallas kernels: 0 us -> 39.8 us
  between operations: 13.9 us -> 0.66 us
  matrix products: 12.9 us -> 0 us
  local copies, waits for them, and re-layouts: 2.51 us -> 7.04 us
    psum x3 -> x0, blocking collectives: 55.3 us -> none  [the longest x1 38.3 us: local(): router_grad = lax.psum(router_part, ('img', 'seq')).astype(jnp.bfloat16)]
    all_gather x4 -> x0, blocking collectives: 44.8 us -> none  [the longest x1 14.1 us: local(): every_in = lax.all_gather(slot_in, 'img', axis=0, tiled=True)]
    psum x1 -> x0, waiting for transfers between devices: 42.5 us -> none  [local(): lax.psum(partial_in.astype(jnp.bfloat16), 'seq').astype(jnp.float32)]
    pallas_call x0 -> x1, Pallas kernels: none -> 39.8 us  [local(): pl.pallas_call(functools.partial(kernel, n_img, n_seq), out_shape=(jax.Sh...]
    reduce_scatter x2 -> x0, waiting for transfers between devices: 39.7 us -> none  [local(): lax.psum_scatter(result.reshape(patches.shape[0] * lax.axis_size('img'),...]
    dot_general x14 -> x0, matrix products: 12.9 us -> none  [the longest x1 2.39 us: local(): jnp.einsum('besf,besd->efd', hidden_grad, grouped, preferred_element_type...]
    pmax x1 -> x0, blocking collectives: 11.5 us -> none  [local(): highest = lax.pmax(jnp.max(logits, axis=1), 'seq')]
    unnamed x16 -> x8, local copies, waits for them, and re-layouts: 1.2 us -> 6.31 us
  transfers between devices with their start and end apart: 3 -> 0, of which waited for: 3 -> 0; matrix products, arithmetic and copies ran while one was open for 2% -> 0% of each run, Pallas kernels for 0% -> 0%
where the time goes in v1:
time: 47.7 us; the launch traced here: 47.5 us
  Pallas kernels  39.8 us (83%)
  local copies, waits for them, and re-layouts  7.04 us (15%)
  between operations  0.66 us (1%)
    pallas_call x1, Pallas kernels, local(): pl.pallas_call(functools.partial(kernel, n_img, n_seq), out_shape=(jax.Sh...  39.8 us
    unnamed x8, local copies, waits for them, and re-layouts  6.31 us

profile of v1, /device:TPU:0, one launch (start us, length us, event | category | flops | bytes accessed | tf_op | source)
XLA Modules:
  0.0 47.5 jit_solution(5911948199222272215)
XLA Ops:
  0.6 1.0 %copy.9.rou_hbm = bf16[512,64]{1,0:T(8,128)(2,1)S(1)} copy(bf16[512,64]{0,1:T(8,128)(2,1)} %param.6) | data formatting | bytes 131072 | tf_op args[1]
  1.6 0.0 copy-start
  1.6 1.2 %copy-done = bf16[1,1024,512]{2,1,0:T(8,128)(2,1)S(1)} copy-done((bf16[1,1024,512]{2,1,0:T(8,128)(2,1)S(1)}, bf16[1,1024,512]{2,1,0:T(8,128)(2,1)}, u32[]{:S(2)}) %copy-start) | copy-done | bytes 1048600
  2.8 0.0 copy-start.1
  2.8 1.2 %copy-done.1 = bf16[2,512,512]{2,1,0:T(8,128)(2,1)S(1)} copy-done((bf16[2,512,512]{2,1,0:T(8,128)(2,1)S(1)}, bf16[2,512,512]{2,1,0:T(8,128)(2,1)}, u32[]{:S(2)}) %copy-start.1) | copy-done | bytes 1048600
  4.0 39.8 %shard_map.84 = (bf16[1,1024,512]{2,1,0:T(8,128)(2,1)S(1)}, bf16[512,64]{1,0:T(8,128)(2,1)S(1)}, bf16[2,512,512]{2,1,0:T(8,128)(2,1)S(1)}, bf16[2,512,512]{2,1,0:T(8,128)(2,1)S(1)}) custom-call(bf16[1,1024,512]{2,1,0:T(8,128)(2,1)S(1)} %copy-done, bf16[512,64]{1,0:T(8,128)(2,1)S(1)} %copy.9.rou_hbm, bf16[2,512,512]{2,1,0:T(8,128)(2,1)S(1)} %copy-done.1, ...), custom_call_target="tpu_custom_call" | custom-call | tf_op jit(solution)/shard_map/pallas_call | solution.py:248
  43.8 0.7 %copy.10 = bf16[512,64]{0,1:T(8,128)(2,1)} copy(bf16[512,64]{1,0:T(8,128)(2,1)S(1)} %get-tuple-element.5) | data formatting | bytes 131072 | tf_op jit(solution)/shard_map/pallas_call | solution.py:248
  44.5 1.0 %copy.14 = bf16[1,1024,512]{2,1,0:T(8,128)(2,1)} copy(bf16[1,1024,512]{2,1,0:T(8,128)(2,1)S(1)} %get-tuple-element.12) | data formatting | bytes 2097152
  45.5 1.0 %copy.15 = bf16[2,512,512]{2,1,0:T(8,128)(2,1)} copy(bf16[2,512,512]{2,1,0:T(8,128)(2,1)S(1)} %get-tuple-element.14) | data formatting | bytes 2097152
  46.5 1.0 %copy.16 = bf16[2,512,512]{2,1,0:T(8,128)(2,1)} copy(bf16[2,512,512]{2,1,0:T(8,128)(2,1)S(1)} %get-tuple-element.15) | data formatting | bytes 2097152
Async XLA Ops:
  1.6 1.2 %copy-start = (bf16[1,1024,512]{2,1,0:T(8,128)(2,1)S(1)}, bf16[1,1024,512]{2,1,0:T(8,128)(2,1)}, u32[]{:S(2)}) copy-start(bf16[1,1024,512]{2,1,0:T(8,128)(2,1)} %pat_hbm.1) | copy-start | bytes 3145732
  2.8 1.2 %copy-start.1 = (bf16[2,512,512]{2,1,0:T(8,128)(2,1)S(1)}, bf16[2,512,512]{2,1,0:T(8,128)(2,1)}, u32[]{:S(2)}) copy-start(bf16[2,512,512]{2,1,0:T(8,128)(2,1)} %win_hbm.1) | copy-start | bytes 3145732

commit v2 on v1

--- a/solution.py
+++ b/solution.py
@@ -58,6 +58,118 @@
             copy.wait_send()
 
 
+class Copies:
+    def __init__(self, send_sem, recv_sem):
+        self.send_sem, self.recv_sem = send_sem, recv_sem
+        self.copies = []
+
+    def send(self, src, dst, device, at):
+        copy = pltpu.make_async_remote_copy(
+            src_ref=src,
+            dst_ref=dst,
+            send_sem=self.send_sem.at[at],
+            recv_sem=self.recv_sem.at[at],
+            device_id=device,
+            device_id_type=MESH,
+        )
+        copy.start()
+        self.copies.append(copy)
+
+    def wait_recv(self):
+        for copy in self.copies:
+            copy.wait_recv()
+
+    def wait_send(self):
+        for copy in self.copies:
+            copy.wait_send()
+
+
+class Relay:
+    def __init__(self, n_img, block, send_sem, recv_sem):
+        img = lax.axis_index("img")
+        self.chips, self.chip, self.core = n_img // 2, img // 2, lax.rem(img, 2)
+        self.block, self.send_sem, self.recv_sem = block, send_sem, recv_sem
+        self.copies = []
+
+    def send(self, owner, peer, at):
+        copy = pltpu.make_async_remote_copy(
+            src_ref=self.block.at[owner],
+            dst_ref=self.block.at[owner],
+            send_sem=self.send_sem.at[at],
+            recv_sem=self.recv_sem.at[at],
+            device_id={"img": peer},
+            device_id_type=MESH,
+        )
+        copy.start()
+        self.copies.append(copy)
+
+    def start(self):
+        own = self.chip * 2 + self.core
+        for step in range(1, self.chips):
+            self.send(own, lax.rem(self.chip + step, self.chips) * 2 + self.core, step - 1)
+        self.send(own, self.chip * 2 + 1 - self.core, self.chips - 1)
+        return self
+
+    def forward(self):
+        for step in range(1, self.chips):
+            self.copies[step - 1].wait_recv()
+            owner = lax.rem(self.chip + self.chips - step, self.chips) * 2 + self.core
+            self.send(owner, self.chip * 2 + 1 - self.core, self.chips - 1 + step)
+
+    def wait_recv(self):
+        for copy in self.copies[self.chips - 1:]:
+            copy.wait_recv()
+
+    def wait_send(self):
+        for copy in self.copies:
+            copy.wait_send()
+
+
+class PairSum:
+    def __init__(self, n_img, own, other, pair, landing, send_sem, recv_sem):
+        img = lax.axis_index("img")
+        self.chips, self.chip, self.core = n_img // 2, img // 2, lax.rem(img, 2)
+        self.own, self.other, self.pair, self.landing = own, other, pair, landing
+        self.send_sem, self.recv_sem = send_sem, recv_sem
+        self.copies = []
+
+    def send(self, src, dst, peer, at):
+        copy = pltpu.make_async_remote_copy(
+            src_ref=src,
+            dst_ref=dst,
+            send_sem=self.send_sem.at[at],
+            recv_sem=self.recv_sem.at[at],
+            device_id={"img": peer},
+            device_id_type=MESH,
+        )
+        copy.start()
+        self.copies.append(copy)
+
+    def start(self, wide):
+        for core in range(2):
+            self.own[core] = wide[:, core]
+        sibling = 1 - self.core
+        self.send(self.own.at[sibling], self.other, self.chip * 2 + sibling, 0)
+        return self
+
+    def middle(self):
+        self.copies[0].wait_recv()
+        self.pair[...] = (self.own[self.core].astype(F32) + self.other[...].astype(F32)).astype(BF)
+        self.landing[self.chip] = self.pair[self.chip]
+        for step in range(1, self.chips):
+            chip = lax.rem(self.chip + step, self.chips)
+            self.send(self.pair.at[chip], self.landing.at[self.chip], chip * 2 + self.core, step)
+
+    def result(self):
+        for copy in self.copies[1:]:
+            copy.wait_recv()
+        return jnp.sum(self.landing[...].astype(F32), axis=0).astype(BF)
+
+    def wait_send(self):
+        for copy in self.copies:
+            copy.wait_send()
+
+
 def kernel(
     n_img, n_seq,
     pat_hbm, rou_hbm, win_hbm, wout_hbm, cot_hbm,
@@ -65,39 +177,55 @@
     pat, rou, win, wout, cot,
     pg, rg, wig, wog,
     a_in_s, a_in_r, a_gr_s, a_gr_r, a_st_s, a_st_r,
-    b_in, b_gr, c_out_s, c_out_r, c_ig_s, c_ig_r,
+    b_in, b_gr, c_out, c_out_x, c_out_p, c_out_r, c_ig, c_ig_x, c_ig_p, c_ig_r,
     d_out, d_ig, d_st, e_s, e_r, f_buf, g_buf,
     act_s, hg_s,
-    load_sem, store_sem, seq_send, seq_recv, img_send, img_recv,
+    load_sem, store_sem, seq_send, seq_recv, img_send, img_recv, plane_send, plane_recv,
 ):
     img, seq = lax.axis_index("img"), lax.axis_index("seq")
     experts = win.shape[0]
     rows, depth = b_in.shape[1], b_in.shape[2]
     slots = n_seq * rows
 
-    loads = []
-    for at, (src, dst) in enumerate(
-        ((pat_hbm.at[0], pat), (rou_hbm, rou), (cot_hbm.at[0], cot), (win_hbm, win), (wout_hbm, wout))
-    ):
-        copy = pltpu.make_async_copy(src, dst, load_sem.at[at])
-        copy.start()
-        loads.append(copy)
+    chips, chip, core = n_img // 2, img // 2, lax.rem(img, 2)
+
+    def plane_peers():
+        own = seq * 2 + core
+        for step in range(1, n_seq * 2):
+            peer = lax.rem(own + step, n_seq * 2)
+            yield step, {"img": chip * 2 + lax.rem(peer, 2), "seq": peer // 2}, peer
+
+    def chip_peers():
+        for step in range(1, chips):
+            yield step, {"img": lax.rem(chip + step, chips) * 2 + core}
 
     barrier = pltpu.get_barrier_semaphore()
-    for step in range(1, n_seq):
-        pl.semaphore_signal(
-            barrier, inc=1, device_id={"seq": lax.rem(seq + step, n_seq)}, device_id_type=MESH
+    for _, device, _ in plane_peers():
+        pl.semaphore_signal(barrier, inc=1, device_id=device, device_id_type=MESH)
+    for _, device in chip_peers():
+        pl.semaphore_signal(barrier, inc=1, device_id=device, device_id_type=MESH)
+
+    loads = [
+        pltpu.make_async_copy(src, dst, load_sem.at[at])
+        for at, (src, dst) in enumerate(
+            ((pat_hbm.at[0], pat), (rou_hbm, rou), (cot_hbm.at[0], cot), (win_hbm, win), (wout_hbm, wout))
         )
-    for step in range(1, n_img):
-        pl.semaphore_signal(
-            barrier, inc=1, device_id={"img": lax.rem(img + step, n_img)}, device_id_type=MESH
-        )
+    ]
+    for copy in loads[:3]:
+        copy.start()
 
     def over_seq(at):
         return Exchange("seq", n_seq, seq_send.at[at], seq_recv.at[at])
 
-    def over_img(at):
-        return Exchange("img", n_img, img_send.at[at], img_recv.at[at])
+    def relay(at, block):
+        exchange = Relay(n_img, block, img_send.at[at], img_recv.at[at])
+        started.append(exchange)
+        return exchange.start()
+
+    def pair_sum(at, wide, *buffers):
+        exchange = PairSum(n_img, *buffers, img_send.at[at], img_recv.at[at])
+        started.append(exchange)
+        return exchange.start(wide)
 
     started = []
 
@@ -107,7 +235,7 @@
         return exchange
 
     loads[1].wait()
-    router_t = rou[...].astype(F32).T.astype(BF)
+    router_t = rou[...]
     loads[0].wait()
     logits = dot(router_t, pat[...], ((1,), (1,)))
     own_max = jnp.max(logits, axis=1, keepdims=True)
@@ -119,9 +247,11 @@
     a_in_s[...] = part_in.astype(BF).reshape(n_seq, rows, depth)
     a_st_r[seq] = a_st_s[seq]
     a_in_r[seq] = a_in_s[seq]
-    pl.semaphore_wait(barrier, n_seq - 1 + n_img - 1)
+    pl.semaphore_wait(barrier, n_seq * 2 - 1 + chips - 1)
     a_st = go(over_seq(0), a_st_s, a_st_r, False)
     a_in = go(over_seq(1), a_in_s, a_in_r, False)
+    for copy in loads[3:]:
+        copy.start()
 
     comb = jnp.exp(logits - jnp.max(logits, axis=0, keepdims=True))
     comb = comb * (1.0 / jnp.sum(comb, axis=0, keepdims=True))
@@ -140,10 +270,10 @@
     total = jnp.sum(shares, axis=0, keepdims=True)
     slot_in = jnp.sum(a_in_r[...].astype(F32) * (shares / total), axis=0)
     b_in[img] = slot_in.astype(BF)
-    g_in = go(over_img(0), b_in, b_in, True)
+    g_in = relay(0, b_in)
     a_gr.wait_recv()
     b_gr[img] = jnp.sum(a_gr_r[...].astype(F32), axis=0).astype(BF)
-    g_gr = go(over_img(1), b_gr, b_gr, True)
+    g_gr = relay(1, b_gr)
 
     def of_expert(buffer, e):
         wide = buffer[...].astype(F32).reshape(n_img, experts, SLOTS, depth)
@@ -151,9 +281,11 @@
 
     def all_rows(parts):
         wide = [part.reshape(n_img, 1, SLOTS, depth) for part in parts]
-        return jnp.concatenate(wide, axis=1).reshape(n_img, rows, depth).astype(BF)
+        wide = jnp.concatenate(wide, axis=1).reshape(n_img // 2, 2, rows, depth)
+        return wide.astype(BF)
 
     loads[3].wait()
+    g_in.forward()
     g_in.wait_recv()
     slopes, parts = [], []
     loads[4].wait()
@@ -163,18 +295,17 @@
         slopes.append(slope)
         act_s[e] = active.astype(BF)
         parts.append(dot(act_s[e], wout[e], ((1,), (0,))))
-    c_out_s[...] = all_rows(parts)
-    c_out_r[img] = c_out_s[img]
-    c_out = go(over_img(2), c_out_s, c_out_r, False)
+    out_sum = pair_sum(2, all_rows(parts), c_out, c_out_x, c_out_p, c_out_r)
+    g_gr.forward()
     g_gr.wait_recv()
     parts = []
     for e in range(experts):
         act_grad = dot(of_expert(b_gr, e), wout[e], ((1,), (1,)))
         hg_s[e] = (act_grad * slopes[e]).astype(BF)
         parts.append(dot(hg_s[e], win[e], ((1,), (0,))))
-    c_ig_s[...] = all_rows(parts)
-    c_ig_r[img] = c_ig_s[img]
-    c_ig = go(over_img(3), c_ig_s, c_ig_r, False)
+    ig_sum = pair_sum(3, all_rows(parts), c_ig, c_ig_x, c_ig_p, c_ig_r)
+    out_sum.middle()
+    ig_sum.middle()
 
     stores = []
 
@@ -187,14 +318,12 @@
         wog[e] = dot(act_s[e], of_expert(b_gr, e), ((0,), (0,))).astype(BF)
     store(wog, wog_hbm)
 
-    c_out.wait_recv()
-    d_out[seq] = jnp.sum(c_out_r[...].astype(F32), axis=0).astype(BF)
+    d_out[seq] = out_sum.result()
     e_out = go(over_seq(3), d_out, d_out, True)
     for e in range(experts):
         wig[e] = dot(hg_s[e], of_expert(b_in, e), ((0,), (0,))).astype(BF)
     store(wig, wig_hbm)
-    c_ig.wait_recv()
-    input_grad = jnp.sum(c_ig_r[...].astype(F32), axis=0).astype(BF)
+    input_grad = ig_sum.result()
     d_ig[seq] = input_grad
     e_ig = go(over_seq(4), d_ig, d_ig, True)
     inner = jnp.sum(slot_in * input_grad.astype(F32), axis=1, keepdims=True)
@@ -215,21 +344,36 @@
     disp = raised * scale
     logit_grad = (disp * (disp_grad - stats[:, INNER_LANE:INNER_LANE + 1]) + comb_part).astype(BF)
 
-    e_s[...] = dot(logit_grad, pat[...], ((1,), (0,))).reshape(n_seq, rows, depth)
-    e_r[seq] = e_s[seq]
-    r_sum = go(over_seq(6), e_s, e_r, False)
+    router_part = dot(logit_grad, pat[...], ((1,), (0,))).reshape(n_seq, rows, depth)
+    half = depth // 2
+    for side in range(2):
+        e_s[:, side] = router_part[:, :, side * half:(side + 1) * half]
+    e_r[seq * 2 + core] = e_s[seq, core]
+
+    def to_plane(at, source, landing):
+        copies = Copies(plane_send.at[at], plane_recv.at[at])
+        for step, device, peer in plane_peers():
+            copies.send(source(peer), landing, device, step)
+        started.append(copies)
+        return copies
+
+    r_sum = to_plane(0, lambda peer: e_s.at[peer // 2, lax.rem(peer, 2)], e_r.at[seq * 2 + core])
     left = jnp.concatenate([logit_grad, disp.astype(BF)], axis=0)
     right = jnp.concatenate([router_t, every_ig], axis=0)
     pg[...] = dot(left, right, ((0,), (0,))).astype(BF)
     store(pg, pg_hbm.at[0])
     r_sum.wait_recv()
-    f_buf[img] = jnp.sum(e_r[...], axis=0).astype(BF)
-    r_all = go(over_img(4), f_buf, f_buf, True)
+    f_buf[chip] = jnp.sum(e_r[...], axis=0)
+    r_all = Copies(img_send.at[4], img_recv.at[4])
+    for step, device in chip_peers():
+        r_all.send(f_buf.at[chip], f_buf.at[chip], device, step)
+    started.append(r_all)
     r_all.wait_recv()
-    g_buf[seq] = jnp.sum(f_buf[...].astype(F32), axis=0).astype(BF)
-    r_back = go(over_seq(7), g_buf, g_buf, True)
-    r_back.wait_recv()
-    rg[...] = g_buf[...].astype(F32).reshape(slots, depth).T.astype(BF)
+    own_block = g_buf.at[seq * 2 + core]
+    own_block[...] = jnp.sum(f_buf[...], axis=0).astype(BF)
+    to_plane(1, lambda peer: own_block, own_block).wait_recv()
+    for at in range(n_seq):
+        rg[at] = jnp.concatenate([g_buf[2 * at], g_buf[2 * at + 1]], axis=1)
     store(rg, rg_hbm)
     for exchange in started:
         exchange.wait_send()
@@ -245,36 +389,40 @@
     any_space = pl.BlockSpec(memory_space=pl.ANY)
     vmem = pltpu.VMEM
     by_seq, by_img = (n_seq, rows, depth), (n_img, rows, depth)
-    return pl.pallas_call(
+    by_chip, half = (n_img // 2, rows, depth), (rows, depth // 2)
+    patch_grad, router_grad, w_in_grad, w_out_grad = pl.pallas_call(
         functools.partial(kernel, n_img, n_seq),
         out_shape=(
             jax.ShapeDtypeStruct(patches.shape, BF),
-            jax.ShapeDtypeStruct(router.shape, BF),
+            jax.ShapeDtypeStruct(by_seq, BF),
             jax.ShapeDtypeStruct(w_in.shape, BF),
             jax.ShapeDtypeStruct(w_out.shape, BF),
         ),
-        in_specs=[any_space] * 5,
+        in_specs=[pl.BlockSpec(memory_space=pltpu.HBM)] * 5,
         out_specs=(any_space,) * 4,
         scratch_shapes=[
-            vmem((count, depth), BF), vmem(router.shape, BF), vmem(w_in.shape, BF),
+            vmem((count, depth), BF), vmem((slots, depth), BF), vmem(w_in.shape, BF),
             vmem(w_out.shape, BF), vmem((count, depth), BF),
-            vmem((count, depth), BF), vmem(router.shape, BF), vmem(w_in.shape, BF),
-            vmem(w_out.shape, BF),
+            vmem((count, depth), BF), vmem(by_seq, BF), vmem(w_in.shape, BF), vmem(w_out.shape, BF),
             vmem(by_seq, BF), vmem(by_seq, BF), vmem(by_seq, BF), vmem(by_seq, BF),
             vmem((n_seq, rows, 128), F32), vmem((n_seq, rows, 128), F32),
-            vmem(by_img, BF), vmem(by_img, BF), vmem(by_img, BF), vmem(by_img, BF),
             vmem(by_img, BF), vmem(by_img, BF),
+            vmem((2,) + by_chip, BF), vmem(by_chip, BF), vmem(by_chip, BF), vmem(by_chip, BF),
+            vmem((2,) + by_chip, BF), vmem(by_chip, BF), vmem(by_chip, BF), vmem(by_chip, BF),
             vmem(by_seq, BF), vmem(by_seq, BF), vmem((n_seq, rows, 128), F32),
-            vmem(by_seq, F32), vmem(by_seq, F32), vmem(by_img, BF), vmem(by_seq, BF),
+            vmem((n_seq, 2) + half, F32), vmem((n_seq * 2,) + half, F32),
+            vmem((n_img // 2,) + half, F32), vmem((n_seq * 2,) + half, BF),
             vmem((experts, n_img * SLOTS, units), BF), vmem((experts, n_img * SLOTS, units), BF),
             pltpu.SemaphoreType.DMA((5,)), pltpu.SemaphoreType.DMA((4,)),
             pltpu.SemaphoreType.DMA((8, n_seq)), pltpu.SemaphoreType.DMA((8, n_seq)),
             pltpu.SemaphoreType.DMA((5, n_img)), pltpu.SemaphoreType.DMA((5, n_img)),
+            pltpu.SemaphoreType.DMA((2, 2 * n_seq)), pltpu.SemaphoreType.DMA((2, 2 * n_seq)),
         ],
         compiler_params=pltpu.CompilerParams(
-            collective_id=0, has_side_effects=True, vmem_limit_bytes=48 * 1024 * 1024
+            collective_id=0, has_side_effects=True, vmem_limit_bytes=60 * 1024 * 1024
         ),
-    )(patches, router, w_in, w_out, cotangent)
+    )(patches, router.T, w_in, w_out, cotangent)
+    return patch_grad, router_grad.reshape(slots, depth).T, w_in_grad, w_out_grad
 
 
 def solution(mesh):

time: 47.7 us -> 45.2 us (0.948)
  local copies, waits for them, and re-layouts: 7.04 us -> 5.56 us
  Pallas kernels: 39.8 us -> 38.8 us
    pallas_call x1, Pallas kernels: 39.8 us -> 38.8 us  [local(): pl.pallas_call(functools.partial(kernel, n_img, n_seq), out_shape=(jax.Sh...]
    unnamed x8 -> x10, local copies, waits for them, and re-layouts: 6.31 us -> 5.56 us
    pallas_call x1 -> x0, local copies, waits for them, and re-layouts: 0.73 us -> none  [local(): pl.pallas_call(functools.partial(kernel, n_img, n_seq), out_shape=(jax.Sh...]
where the time goes in v2:
time: 45.2 us; the launch traced here: 45 us
  Pallas kernels  38.8 us (86%)
  local copies, waits for them, and re-layouts  5.56 us (12%)
  between operations  0.66 us (1%)
    pallas_call x1, Pallas kernels, local(): pl.pallas_call(functools.partial(kernel, n_img, n_seq), out_shape=(jax.Sh...  38.8 us
    unnamed x10, local copies, waits for them, and re-layouts  5.56 us

profile of v2, /device:TPU:0, one launch (start us, length us, event | category | flops | bytes accessed | tf_op | source)
XLA Modules:
  0.0 45.0 jit_solution(8116526223300797026)
XLA Ops:
  0.6 38.8 %shard_map.84 = (bf16[1,1024,512]{2,1,0:T(8,128)(2,1)}, bf16[4,16,512]{2,1,0:T(8,128)(2,1)}, bf16[2,512,512]{2,1,0:T(8,128)(2,1)}, bf16[2,512,512]{2,1,0:T(8,128)(2,1)}) custom-call(bf16[1,1024,512]{2,1,0:T(8,128)(2,1)} %pat_hbm.1, bf16[64,512]{1,0:T(8,128)(2,1)} %bitcast.4, bf16[2,512,512]{2,1,0:T(8,128)(2,1)} %win_hbm.1, bf16[2,512,512]{2,1,0:T(8,128)(2,1)} %wout_hbm.1, ...), custom_call_target="tpu_custom_call" | custom-call | tf_op jit(solution)/shard_map/pallas_call | solution.py:393
  39.4 0.0 copy-start.2
  39.4 0.0 copy-start.1
  39.4 2.4 %copy.13 = bf16[1,1024,512]{2,1,0:T(8,128)(2,1)} copy(bf16[1,1024,512]{2,1,0:T(8,128)(2,1)} %get-tuple-element.16) | data formatting | bytes 2097152
  41.8 0.0 copy-done.2
  41.8 0.6 %copy.14 = bf16[512,64]{0,1:T(8,128)(2,1)} copy(bf16[512,64]{0,1:T(8,128)(2,1)S(1)} %bitcast.5) | data formatting | bytes 131072
  42.4 0.0 copy-done.1
  42.4 0.0 copy-start
  42.4 1.0 %copy.15 = bf16[2,512,512]{2,1,0:T(8,128)(2,1)} copy(bf16[2,512,512]{2,1,0:T(8,128)(2,1)S(1)} %copy-done.1) | data formatting | bytes 2097152
  43.4 0.6 %copy-done = bf16[2,512,512]{2,1,0:T(8,128)(2,1)S(1)} copy-done((bf16[2,512,512]{2,1,0:T(8,128)(2,1)S(1)}, bf16[2,512,512]{2,1,0:T(8,128)(2,1)}, u32[]{:S(2)}) %copy-start) | copy-done | bytes 1048600
  44.0 1.0 %copy.16 = bf16[2,512,512]{2,1,0:T(8,128)(2,1)} copy(bf16[2,512,512]{2,1,0:T(8,128)(2,1)S(1)} %copy-done) | data formatting | bytes 2097152
Async XLA Ops:
  39.4 2.4 %copy-start.2 = (bf16[4,16,512]{2,1,0:T(8,128)(2,1)S(1)}, bf16[4,16,512]{2,1,0:T(8,128)(2,1)}, u32[]{:S(2)}) copy-start(bf16[4,16,512]{2,1,0:T(8,128)(2,1)} %get-tuple-element.9) | copy-start | bytes 196612
  39.4 3.0 %copy-start.1 = (bf16[2,512,512]{2,1,0:T(8,128)(2,1)S(1)}, bf16[2,512,512]{2,1,0:T(8,128)(2,1)}, u32[]{:S(2)}) copy-start(bf16[2,512,512]{2,1,0:T(8,128)(2,1)} %get-tuple-element.18) | copy-start | bytes 3145732
  42.4 1.6 %copy-start = (bf16[2,512,512]{2,1,0:T(8,128)(2,1)S(1)}, bf16[2,512,512]{2,1,0:T(8,128)(2,1)}, u32[]{:S(2)}) copy-start(bf16[2,512,512]{2,1,0:T(8,128)(2,1)} %get-tuple-element.19) | copy-start | bytes 3145732

commit v3 on v2

--- a/solution.py
+++ b/solution.py
@@ -12,6 +12,7 @@
 MESH = pl.DeviceIdType.MESH
 BF = jnp.bfloat16
 F32 = jnp.float32
+CHUNK = 256
 MAX_LANE, TOTAL_LANE, INNER_LANE = 0, 1, 2
 
 
@@ -58,6 +59,12 @@
             copy.wait_send()
 
 
+def of_expert(buffer, e, experts):
+    n_img, rows, depth = buffer.shape
+    wide = buffer[...].astype(F32).reshape(n_img, experts, SLOTS, depth)
+    return wide[:, e].reshape(n_img * SLOTS, depth).astype(BF)
+
+
 class Copies:
     def __init__(self, send_sem, recv_sem):
         self.send_sem, self.recv_sem = send_sem, recv_sem
@@ -173,9 +180,9 @@
 def kernel(
     n_img, n_seq,
     pat_hbm, rou_hbm, win_hbm, wout_hbm, cot_hbm,
-    pg_hbm, rg_hbm, wig_hbm, wog_hbm,
+    left_hbm, right_hbm, rg_hbm, act_hbm, hg_hbm, in_hbm, gr_hbm,
     pat, rou, win, wout, cot,
-    pg, rg, wig, wog,
+    left, right, rg,
     a_in_s, a_in_r, a_gr_s, a_gr_r, a_st_s, a_st_r,
     b_in, b_gr, c_out, c_out_x, c_out_p, c_out_r, c_ig, c_ig_x, c_ig_p, c_ig_r,
     d_out, d_ig, d_st, e_s, e_r, f_buf, g_buf,
@@ -275,10 +282,6 @@
     b_gr[img] = jnp.sum(a_gr_r[...].astype(F32), axis=0).astype(BF)
     g_gr = relay(1, b_gr)
 
-    def of_expert(buffer, e):
-        wide = buffer[...].astype(F32).reshape(n_img, experts, SLOTS, depth)
-        return wide[:, e].reshape(n_img * SLOTS, depth).astype(BF)
-
     def all_rows(parts):
         wide = [part.reshape(n_img, 1, SLOTS, depth) for part in parts]
         wide = jnp.concatenate(wide, axis=1).reshape(n_img // 2, 2, rows, depth)
@@ -290,7 +293,7 @@
     slopes, parts = [], []
     loads[4].wait()
     for e in range(experts):
-        hidden = dot(of_expert(b_in, e), win[e], ((1,), (1,)))
+        hidden = dot(of_expert(b_in, e, experts), win[e], ((1,), (1,)))
         active, slope = gelu_and_slope(hidden)
         slopes.append(slope)
         act_s[e] = active.astype(BF)
@@ -300,7 +303,7 @@
     g_gr.wait_recv()
     parts = []
     for e in range(experts):
-        act_grad = dot(of_expert(b_gr, e), wout[e], ((1,), (1,)))
+        act_grad = dot(of_expert(b_gr, e, experts), wout[e], ((1,), (1,)))
         hg_s[e] = (act_grad * slopes[e]).astype(BF)
         parts.append(dot(hg_s[e], win[e], ((1,), (0,))))
     ig_sum = pair_sum(3, all_rows(parts), c_ig, c_ig_x, c_ig_p, c_ig_r)
@@ -314,15 +317,13 @@
         copy.start()
         stores.append(copy)
 
-    for e in range(experts):
-        wog[e] = dot(act_s[e], of_expert(b_gr, e), ((0,), (0,))).astype(BF)
-    store(wog, wog_hbm)
+    store(act_s, act_hbm)
+    store(hg_s, hg_hbm)
+    store(b_in, in_hbm)
+    store(b_gr, gr_hbm)
 
     d_out[seq] = out_sum.result()
     e_out = go(over_seq(3), d_out, d_out, True)
-    for e in range(experts):
-        wig[e] = dot(hg_s[e], of_expert(b_in, e), ((0,), (0,))).astype(BF)
-    store(wig, wig_hbm)
     input_grad = ig_sum.result()
     d_ig[seq] = input_grad
     e_ig = go(over_seq(4), d_ig, d_ig, True)
@@ -358,10 +359,12 @@
         return copies
 
     r_sum = to_plane(0, lambda peer: e_s.at[peer // 2, lax.rem(peer, 2)], e_r.at[seq * 2 + core])
-    left = jnp.concatenate([logit_grad, disp.astype(BF)], axis=0)
-    right = jnp.concatenate([router_t, every_ig], axis=0)
-    pg[...] = dot(left, right, ((0,), (0,))).astype(BF)
-    store(pg, pg_hbm.at[0])
+    left[:slots] = logit_grad
+    left[slots:] = disp.astype(BF)
+    right[:slots] = router_t
+    right[slots:] = every_ig
+    store(left, left_hbm)
+    store(right, right_hbm)
     r_sum.wait_recv()
     f_buf[chip] = jnp.sum(e_r[...], axis=0)
     r_all = Copies(img_send.at[4], img_recv.at[4])
@@ -381,29 +384,78 @@
         copy.wait()
 
 
+def write_kernel(
+    left_hbm, right_hbm, rg_hbm, act_hbm, hg_hbm, in_hbm, gr_hbm,
+    pg_out, rg_out, wig_out, wog_out,
+    left, right, rg_in, act, hg, b_in, b_gr,
+    pg, rg, wig, wog,
+    load_sem, store_sem,
+):
+    experts, count = act.shape[0], left.shape[1]
+    sources = (left_hbm, right_hbm, act_hbm, gr_hbm, hg_hbm, in_hbm, rg_hbm)
+    loads = [
+        pltpu.make_async_copy(src, dst, load_sem.at[at])
+        for at, (src, dst) in enumerate(zip(sources, (left, right, act, b_gr, hg, b_in, rg_in)))
+    ]
+    for copy in loads:
+        copy.start()
+    stores = []
+
+    def store(src, dst):
+        copy = pltpu.make_async_copy(src, dst, store_sem.at[len(stores)])
+        copy.start()
+        stores.append(copy)
+
+    loads[0].wait()
+    loads[1].wait()
+    for at in range(0, count, CHUNK):
+        span = pl.ds(at, CHUNK)
+        pg[span] = dot(left[:, span], right[...], ((0,), (0,))).astype(BF)
+        store(pg.at[span], pg_out.at[0, span])
+    loads[2].wait()
+    loads[3].wait()
+    for e in range(experts):
+        wog[e] = dot(act[e], of_expert(b_gr, e, experts), ((0,), (0,))).astype(BF)
+        store(wog.at[e], wog_out.at[e])
+    loads[4].wait()
+    loads[5].wait()
+    for e in range(experts):
+        wig[e] = dot(hg[e], of_expert(b_in, e, experts), ((0,), (0,))).astype(BF)
+        store(wig.at[e], wig_out.at[e])
+    loads[6].wait()
+    rg[...] = rg_in[...].reshape(rg.shape)
+    store(rg, rg_out)
+    for copy in stores:
+        copy.wait()
+
+
 def local(n_img, n_seq, patches, router, w_in, w_out, cotangent):
     _, count, depth = patches.shape
     experts, units, _ = w_in.shape
     rows = experts * SLOTS
     slots = n_seq * rows
-    any_space = pl.BlockSpec(memory_space=pl.ANY)
+    by_unit = (experts, n_img * SLOTS, units)
+    any_space = pl.BlockSpec(memory_space=pltpu.HBM)
     vmem = pltpu.VMEM
     by_seq, by_img = (n_seq, rows, depth), (n_img, rows, depth)
     by_chip, half = (n_img // 2, rows, depth), (rows, depth // 2)
-    patch_grad, router_grad, w_in_grad, w_out_grad = pl.pallas_call(
+    parts = pl.pallas_call(
         functools.partial(kernel, n_img, n_seq),
         out_shape=(
-            jax.ShapeDtypeStruct(patches.shape, BF),
+            jax.ShapeDtypeStruct((2 * slots, count), BF),
+            jax.ShapeDtypeStruct((2 * slots, depth), BF),
             jax.ShapeDtypeStruct(by_seq, BF),
-            jax.ShapeDtypeStruct(w_in.shape, BF),
-            jax.ShapeDtypeStruct(w_out.shape, BF),
+            jax.ShapeDtypeStruct(by_unit, BF),
+            jax.ShapeDtypeStruct(by_unit, BF),
+            jax.ShapeDtypeStruct(by_img, BF),
+            jax.ShapeDtypeStruct(by_img, BF),
         ),
-        in_specs=[pl.BlockSpec(memory_space=pltpu.HBM)] * 5,
-        out_specs=(any_space,) * 4,
+        in_specs=[any_space] * 5,
+        out_specs=(any_space,) * 7,
         scratch_shapes=[
             vmem((count, depth), BF), vmem((slots, depth), BF), vmem(w_in.shape, BF),
             vmem(w_out.shape, BF), vmem((count, depth), BF),
-            vmem((count, depth), BF), vmem(by_seq, BF), vmem(w_in.shape, BF), vmem(w_out.shape, BF),
+            vmem((2 * slots, count), BF), vmem((2 * slots, depth), BF), vmem(by_seq, BF),
             vmem(by_seq, BF), vmem(by_seq, BF), vmem(by_seq, BF), vmem(by_seq, BF),
             vmem((n_seq, rows, 128), F32), vmem((n_seq, rows, 128), F32),
             vmem(by_img, BF), vmem(by_img, BF),
@@ -412,8 +464,8 @@
             vmem(by_seq, BF), vmem(by_seq, BF), vmem((n_seq, rows, 128), F32),
             vmem((n_seq, 2) + half, F32), vmem((n_seq * 2,) + half, F32),
             vmem((n_img // 2,) + half, F32), vmem((n_seq * 2,) + half, BF),
-            vmem((experts, n_img * SLOTS, units), BF), vmem((experts, n_img * SLOTS, units), BF),
-            pltpu.SemaphoreType.DMA((5,)), pltpu.SemaphoreType.DMA((4,)),
+            vmem(by_unit, BF), vmem(by_unit, BF),
+            pltpu.SemaphoreType.DMA((5,)), pltpu.SemaphoreType.DMA((7,)),
             pltpu.SemaphoreType.DMA((8, n_seq)), pltpu.SemaphoreType.DMA((8, n_seq)),
             pltpu.SemaphoreType.DMA((5, n_img)), pltpu.SemaphoreType.DMA((5, n_img)),
             pltpu.SemaphoreType.DMA((2, 2 * n_seq)), pltpu.SemaphoreType.DMA((2, 2 * n_seq)),
@@ -422,7 +474,25 @@
             collective_id=0, has_side_effects=True, vmem_limit_bytes=60 * 1024 * 1024
         ),
     )(patches, router.T, w_in, w_out, cotangent)
-    return patch_grad, router_grad.reshape(slots, depth).T, w_in_grad, w_out_grad
+    patch_grad, router_grad, w_in_grad, w_out_grad = pl.pallas_call(
+        write_kernel,
+        out_shape=(
+            jax.ShapeDtypeStruct(patches.shape, BF),
+            jax.ShapeDtypeStruct((slots, depth), BF),
+            jax.ShapeDtypeStruct(w_in.shape, BF),
+            jax.ShapeDtypeStruct(w_out.shape, BF),
+        ),
+        in_specs=[any_space] * 7,
+        out_specs=(any_space,) * 4,
+        scratch_shapes=[
+            vmem((2 * slots, count), BF), vmem((2 * slots, depth), BF), vmem(by_seq, BF),
+            vmem(by_unit, BF), vmem(by_unit, BF), vmem(by_img, BF), vmem(by_img, BF),
+            vmem((count, depth), BF), vmem((slots, depth), BF), vmem(w_in.shape, BF), vmem(w_out.shape, BF),
+            pltpu.SemaphoreType.DMA((7,)), pltpu.SemaphoreType.DMA((3 + 2 * experts + count // CHUNK,)),
+        ],
+        compiler_params=pltpu.CompilerParams(vmem_limit_bytes=60 * 1024 * 1024),
+    )(*parts)
+    return patch_grad, router_grad.T, w_in_grad, w_out_grad
 
 
 def solution(mesh):

time: 45.2 us -> 42.9 us (0.949)
  local copies, waits for them, and re-layouts: 5.56 us -> 0 us
  Pallas kernels: 38.8 us -> 42.1 us
    unnamed x10 -> x0, local copies, waits for them, and re-layouts: 5.56 us -> none
    pallas_call x0 -> x1, Pallas kernels: none -> 3.36 us  [local(): pl.pallas_call(write_kernel, out_shape=(jax.ShapeDtypeStruct(patches.shap...]
where the time goes in v3:
time: 42.9 us; the launch traced here: 42.7 us
  Pallas kernels  42.1 us (98%)
  between operations  0.64 us (1%)
    pallas_call x1, Pallas kernels, local(): pl.pallas_call(functools.partial(kernel, n_img, n_seq), out_shape=(jax.Sh...  38.7 us
    pallas_call x1, Pallas kernels, local(): pl.pallas_call(write_kernel, out_shape=(jax.ShapeDtypeStruct(patches.shap...  3.36 us

profile of v3, /device:TPU:0, one launch (start us, length us, event | category | flops | bytes accessed | tf_op | source)
XLA Modules:
  0.0 42.7 jit_solution(303484213870475677)
XLA Ops:
  0.6 38.7 %shard_map.84 = (bf16[128,1024]{1,0:T(8,128)(2,1)}, bf16[128,512]{1,0:T(8,128)(2,1)}, bf16[4,16,512]{2,1,0:T(8,128)(2,1)}, bf16[2,64,512]{2,1,0:T(8,128)(2,1)}, ...) custom-call(bf16[1,1024,512]{2,1,0:T(8,128)(2,1)} %pat_hbm.1, ...), custom_call_target="tpu_custom_call" | custom-call | tf_op jit(solution)/shard_map/pallas_call | solution.py:442
  39.4 3.4 %shard_map.85 = (bf16[1,1024,512]{2,1,0:T(8,128)(2,1)}, bf16[64,512]{1,0:T(8,128)(2,1)}, bf16[2,512,512]{2,1,0:T(8,128)(2,1)}, bf16[2,512,512]{2,1,0:T(8,128)(2,1)}) custom-call(bf16[128,1024]{1,0:T(8,128)(2,1)} %get-tuple-element.15.left_hbm, bf16[128,512]{1,0:T(8,128)(2,1)} %get-tuple-element.16.right_hbm, bf16[4,16,512]{2,1,0:T(8,128)(2,1)} %get-tuple-element.17.rg_hbm, ...), custom_call_target="tpu_custom_call" | custom-call | tf_op jit(solution)/shard_map/pallas_call | solution.py:477

commit v4 on v3

--- a/solution.py
+++ b/solution.py
@@ -289,6 +289,7 @@
 
     loads[3].wait()
     g_in.forward()
+    g_gr.forward()
     g_in.wait_recv()
     slopes, parts = [], []
     loads[4].wait()
@@ -299,7 +300,6 @@
         act_s[e] = active.astype(BF)
         parts.append(dot(act_s[e], wout[e], ((1,), (0,))))
     out_sum = pair_sum(2, all_rows(parts), c_out, c_out_x, c_out_p, c_out_r)
-    g_gr.forward()
     g_gr.wait_recv()
     parts = []
     for e in range(experts):

time: 42.9 us -> 42.1 us (0.981)
  Pallas kernels: 42.1 us -> 41.3 us
    pallas_call x1, Pallas kernels: 38.7 us -> 37.9 us  [local(): pl.pallas_call(functools.partial(kernel, n_img, n_seq), out_shape=(jax.Sh...]
where the time goes in v4:
time: 42.1 us; the launch traced here: 41.9 us
  Pallas kernels  41.3 us (98%)
  between operations  0.64 us (2%)
    pallas_call x1, Pallas kernels, local(): pl.pallas_call(functools.partial(kernel, n_img, n_seq), out_shape=(jax.Sh...  37.9 us
    pallas_call x1, Pallas kernels, local(): pl.pallas_call(write_kernel, out_shape=(jax.ShapeDtypeStruct(patches.shap...  3.36 us

profile of v4, /device:TPU:0, one launch (start us, length us, event | category | flops | bytes accessed | tf_op | source)
XLA Modules:
  0.0 41.9 jit_solution(12898860281102277226)
XLA Ops:
  0.6 37.9 %shard_map.84 = (bf16[128,1024]{1,0:T(8,128)(2,1)}, bf16[128,512]{1,0:T(8,128)(2,1)}, bf16[4,16,512]{2,1,0:T(8,128)(2,1)}, bf16[2,64,512]{2,1,0:T(8,128)(2,1)}, ...) custom-call(bf16[1,1024,512]{2,1,0:T(8,128)(2,1)} %pat_hbm.1, ...), custom_call_target="tpu_custom_call" | custom-call | tf_op jit(solution)/shard_map/pallas_call | solution.py:442
  38.5 3.4 %shard_map.85 = (bf16[1,1024,512]{2,1,0:T(8,128)(2,1)}, bf16[64,512]{1,0:T(8,128)(2,1)}, bf16[2,512,512]{2,1,0:T(8,128)(2,1)}, bf16[2,512,512]{2,1,0:T(8,128)(2,1)}) custom-call(bf16[128,1024]{1,0:T(8,128)(2,1)} %get-tuple-element.15.left_hbm, bf16[128,512]{1,0:T(8,128)(2,1)} %get-tuple-element.16.right_hbm, bf16[4,16,512]{2,1,0:T(8,128)(2,1)} %get-tuple-element.17.rg_hbm, ...), custom_call_target="tpu_custom_call" | custom-call | tf_op jit(solution)/shard_map/pallas_call | solution.py:477
